TPU v7x, 32 devices: a whole 2x2x4 slice. The times are simulated.
32 devices in a mesh: ep: 8 (over z, x), tp: 4 (over y, core).
Axes of the slice: x: 2, y: 2, z: 4, core: 2. Of those that a mesh axis runs over, the one named last changes fastest.
Arguments:
- tokens: bfloat16 [2048, 3584], P('ep', 'tp'), may hold values from -6 to 6
- grad_out: bfloat16 [2048, 3584], P('ep', 'tp'), may hold values from -6 to 6
- route_ids: int32 [2048, 2], P('ep'), may hold values from 0 to 7, all different within a row; in each aligned block of 256 rows (0 to 255, 256 to 511, ...) at most 128 rows name the same one
- route_probs: float32 [2048, 2], P('ep'), may hold values from 0.2 to 1
- w_gate: bfloat16 [8, 3584, 1024], P('ep', None, 'tp'), may hold values from -0.09375 to 0.09375
- w_up: bfloat16 [8, 3584, 1024], P('ep', None, 'tp'), may hold values from -0.09375 to 0.09375
- w_down: bfloat16 [8, 1024, 3584], P('ep', 'tp'), may hold values from -0.1875 to 0.1875
Outputs:
- grad_tokens: bfloat16 [2048, 3584], P('ep', 'tp')
- grad_gate: bfloat16 [8, 3584, 1024], P('ep', None, 'tp')
- grad_up: bfloat16 [8, 3584, 1024], P('ep', None, 'tp')
- grad_down: bfloat16 [8, 1024, 3584], P('ep', 'tp')
Inputs may be any that keep to these rules, and one draw needn't show every extreme that they name: `route_ids`: each token names 2 different experts. Among the tokens of one index of ep (aligned blocks of 256 tokens), no expert is named by more than 128 tokens, and in every draw some expert is named by exactly 128 of some block.
All inputs are finite; a program needn't handle non-finite values.
Results may differ from a plain program's by a relative error of at most 0.0065.
Values may be sent and summed in bfloat16 or wider, within the bound.
A program may use at most 128 MiB of HBM per device.

v0:
```python
import jax
import jax.numpy as jnp
from jax import lax
from jax.sharding import PartitionSpec as P


def contract_last(left, right):
    return lax.dot_general(
        left, right, (((1,), (1,)), ((), ())), preferred_element_type=jnp.float32
    )


def contract_first(left, right):
    return lax.dot_general(
        left, right, (((0,), (0,)), ((), ())), preferred_element_type=jnp.float32
    )


def row_pass(x_rows, s_rows, gate_cols, up_cols, down_rows):
    gate = jnp.dot(x_rows, gate_cols, preferred_element_type=jnp.float32)
    upper = jnp.dot(x_rows, up_cols, preferred_element_type=jnp.float32)
    sigma = jax.nn.sigmoid(gate)
    active = gate * sigma
    hidden = (active * upper).astype(jnp.bfloat16)
    back = contract_last(s_rows, down_rows)
    d_up = (back * active).astype(jnp.bfloat16)
    d_gate = (back * upper * sigma * (1.0 + gate * (1.0 - sigma))).astype(jnp.bfloat16)
    return (
        d_gate,
        d_up,
        contract_first(x_rows, d_gate),
        contract_first(x_rows, d_up),
        contract_first(hidden, s_rows),
    )


def per_device(tokens, grad_out, route_ids, route_probs, w_gate, w_up, w_down):
    n_src = lax.axis_size("ep")
    tok_rows, quarter = tokens.shape
    top = route_ids.shape[1]
    width = w_gate.shape[1]
    cap = max(2, 2 * tok_rows * top // n_src)
    total_rows = n_src * cap
    gate_cols = w_gate[0]
    up_cols = w_up[0]
    down_rows = w_down[0]
    flat_ids = route_ids.reshape(-1)
    routes = flat_ids.shape[0]
    onehot = (flat_ids[:, None] == jnp.arange(n_src, dtype=jnp.int32)[None, :]).astype(jnp.int32)
    rank = jnp.sum((jnp.cumsum(onehot, axis=0) - onehot) * onehot, axis=1)
    slot = flat_ids * cap + rank
    route_of = (
        jnp.full((n_src * cap,), routes, jnp.int32)
        .at[slot]
        .set(jnp.arange(routes, dtype=jnp.int32))
    )
    filled = route_of < routes
    token_of = jnp.where(filled, route_of // top, tok_rows)
    x_send = jnp.take(tokens, token_of, axis=0, mode="fill", fill_value=0).reshape(
        n_src, cap, quarter
    )
    scaled = (route_probs[:, :, None] * grad_out[:, None, :].astype(jnp.float32)).astype(
        jnp.bfloat16
    )
    s_send = jnp.take(
        scaled.reshape(routes, quarter), route_of, axis=0, mode="fill", fill_value=0
    ).reshape(n_src, cap, quarter)
    x_recv, s_recv = (
        lax.all_to_all(x_send, "ep", split_axis=0, concat_axis=0, tiled=True),
        lax.all_to_all(s_send, "ep", split_axis=0, concat_axis=0, tiled=True),
    )
    x_full, s_full = (
        lax.all_gather(x_recv, "tp", axis=2, tiled=True),
        lax.all_gather(s_recv, "tp", axis=2, tiled=True),
    )
    x_rows = x_full.reshape(total_rows, width)
    s_rows = s_full.reshape(total_rows, width)
    d_gate, d_up, g_gate, g_up, g_down = row_pass(x_rows, s_rows, gate_cols, up_cols, down_rows)
    gate_block, up_block = (
        lax.all_to_all(gate_cols, "tp", split_axis=0, concat_axis=1, tiled=True),
        lax.all_to_all(up_cols, "tp", split_axis=0, concat_axis=1, tiled=True),
    )
    dx_rows = contract_last(
        lax.all_gather(d_gate, "tp", axis=1, tiled=True), gate_block
    ) + contract_last(lax.all_gather(d_up, "tp", axis=1, tiled=True), up_block)
    dx_rows = dx_rows.astype(jnp.bfloat16)
    back_slots = lax.all_to_all(
        dx_rows.reshape(n_src, cap, quarter), "ep", split_axis=0, concat_axis=0, tiled=True
    )
    per_route = jnp.take(back_slots.reshape(n_src * cap, quarter), slot, axis=0)
    grad_tokens = jnp.sum(
        per_route.reshape(tok_rows, top, quarter).astype(jnp.float32), axis=1
    ).astype(jnp.bfloat16)
    return (
        grad_tokens,
        g_gate.astype(jnp.bfloat16)[None],
        g_up.astype(jnp.bfloat16)[None],
        g_down.astype(jnp.bfloat16)[None],
    )


def solution(mesh):
    placed = (
        P("ep", "tp"),
        P("ep", "tp"),
        P("ep", None),
        P("ep", None),
        P("ep", None, "tp"),
        P("ep", None, "tp"),
        P("ep", "tp", None),
    )
    return jax.shard_map(
        per_device,
        mesh=mesh,
        in_specs=placed,
        out_specs=(P("ep", "tp"), P("ep", None, "tp"), P("ep", None, "tp"), P("ep", "tp", None)),
        check_vma=False,
    )
```

profile of v0, /device:TPU:0, one launch (start us, length us, event | category | flops | bytes accessed | tf_op | source)
XLA Modules:
  0.0 346.8 jit_solution(9864429461942337807)
XLA Ops:
  7.2 0.0 copy-start
  7.2 0.0 copy-start.2
  7.2 0.0 all-gather.7.cloned.1.call-start
  7.2 0.9 broadcast_multiply_fusion
  8.1 0.8 copy.22
  8.9 0.1 eq.26
  9.1 0.1 reshape.121
  9.2 0.1 copy.26
  9.3 0.1 mul.64
  9.5 1.1 reduce-window.6
  10.7 0.2 slice_reduce_fusion
  10.9 0.1 fusion.13
  11.0 2.4 scatter_custom_fusion
  13.5 5.3 %gather_fusion.1 = bf16[1024,896]{1,0:T(8,128)(2,1)} fusion(bf16[256,896]{1,0:T(8,128)(2,1)S(1)} %copy-done.2, s32[1024]{0:T(1024)S(1)} %get-tuple-element.9), kind=kCustom, calls=%fused_computation.1 | custom fusion | bytes 3674112 | tf_op jit(solution)/shard_map/jit(_take)/gather | solution.py:59
  18.8 1.8 broadcast_select_fusion
  20.6 49.8 %all_to_all.53 = bf16[8,128,896]{2,1,0:T(8,128)(2,1)} all-to-all(bf16[8,128,896]{2,1,0:T(8,128)(2,1)S(1)} %broadcast_select_fusion), channel_id=1, replica_groups=mesh['ep'=8,'tp'=4] {'ep'}, dimensions={0} | all-to-all | bytes 3670016 | tf_op jit(solution)/shard_map/all_to_all | solution.py:69
  70.4 0.0 all-gather.7.cloned.1.call-update
  70.4 0.0 all-gather.5.cloned.1.call-start
  70.4 0.6 copy-done.9
  71.0 0.1 copy.27
  71.2 0.1 mul.65
  71.3 0.1 copy-done.7
  71.4 1.7 mul.67
  73.1 3.4 mul.68
  76.5 1.9 multiply_convert_fusion
  78.5 5.3 %gather_fusion = bf16[1024,896]{1,0:T(8,128)(2,1)} fusion(bf16[512,896]{1,0:T(8,128)(2,1)S(1)} %multiply_convert_fusion, s32[1024]{0:T(1024)S(1)} %get-tuple-element.8), kind=kCustom, calls=%fused_computation | custom fusion | bytes 3674112 | tf_op jit(solution)/shard_map/jit(_take)/gather | solution.py:65
  83.7 1.8 broadcast_select_fusion.1
  85.5 45.7 %all_to_all.54 = bf16[8,128,896]{2,1,0:T(8,128)(2,1)} all-to-all(bf16[8,128,896]{2,1,0:T(8,128)(2,1)S(1)} %broadcast_select_fusion.1), channel_id=1, replica_groups=mesh['ep'=8,'tp'=4] {'ep'}, dimensions={0} | all-to-all | bytes 3670016 | tf_op jit(solution)/shard_map/all_to_all | solution.py:70
  131.3 0.0 all-gather.5.cloned.1.call-update
  131.3 0.0 all-gather.9.cloned.1.call-start
  131.3 0.0 all-gather.7.cloned.1.call-done
  131.4 0.0 copy-start.3
  131.4 6.8 %fusion.3 = f32[1024,256]{1,0:T(8,128)} fusion(bf16[1024,3584]{1,0:T(8,128)(2,1)} %bitcast.66, bf16[1,3584,256]{2,1,0:T(8,128)(2,1)} %param.11), kind=kOutput, calls=%fused_computation.11 | convolution fusion | flops 1879048192 | bytes 10223616 | tf_op jit(solution)/shard_map/dot_general | solution.py:20
  138.2 0.0 copy-done.3
  138.2 0.0 copy-done.10
  138.2 3.0 fusion.5
  141.2 41.5 %all-gather.5.cloned.1.call-done = bf16[8,128,3584]{2,1,0:T(8,128)(2,1)} async-done(((bf16[8,128,896]{2,1,0:T(8,128)(2,1)}), bf16[8,128,3584]{2,1,0:T(8,128)(2,1)}) %all-gather.5.cloned.1.call-update) | async-done | bytes 7340048 | tf_op jit(solution)/shard_map/all_gather | solution.py:74
  182.7 6.9 %multiply_convert_fusion.2 = (bf16[1024,256]{1,0:T(8,128)(2,1)}, bf16[1024,256]{1,0:T(8,128)(2,1)}) fusion(f32[1024,256]{1,0:T(8,128)} %fusion.3, f32[1024,256]{1,0:T(8,128)} %fusion.5, bf16[1024,3584]{1,0:T(8,128)(2,1)} %bitcast.70, bf16[1,256,3584]{2,1,0:T(8,128)(2,1)S(1)} %copy-done), kind=kOutput, calls=%fused_computation.22 | convolution fusion | flops 1882456064 | bytes 12320768 | tf_op jit(solution)/shard_map/dot_general | solution.py:8
  189.6 0.0 all-gather.9.cloned.1.call-update
  189.6 3.6 %all-to-all-start.3 = ((bf16[4,896,256]{2,1,0:T(8,128)(2,1)}), bf16[4,896,256]{2,1,0:T(8,128)(2,1)S(1)}, u32[]{:S(2)}, u32[]{:S(2)}) async-start(bf16[4,896,256]{2,1,0:T(8,128)(2,1)} %bitcast.59), calls=%async_computation.3 | async-start | bytes 3670016 | tf_op jit(solution)/shard_map/all_to_all | solution.py:81
  193.2 0.0 all-gather.11.cloned.1.call-start
  193.3 0.5 all-gather.11.cloned.1.call-update
  193.8 33.5 %all-to-all-done.3 = bf16[4,896,256]{2,1,0:T(8,128)(2,1)S(1)} async-done(((bf16[4,896,256]{2,1,0:T(8,128)(2,1)}), bf16[4,896,256]{2,1,0:T(8,128)(2,1)S(1)}, u32[]{:S(2)}, u32[]{:S(2)}) %all-to-all-start.3) | async-done | bytes 1835040 | tf_op jit(solution)/shard_map/all_to_all | solution.py:81
  227.3 4.6 %all-to-all-start.2 = ((bf16[4,896,256]{2,1,0:T(8,128)(2,1)}), bf16[4,896,256]{2,1,0:T(8,128)(2,1)}, u32[]{:S(2)}, u32[]{:S(2)}) async-start(bf16[4,896,256]{2,1,0:T(8,128)(2,1)} %bitcast.60), calls=%async_computation.2 | async-start | bytes 3670016 | tf_op jit(solution)/shard_map/all_to_all | solution.py:80
  231.9 2.3 copy.29
  234.2 31.7 %all-to-all-done.2 = bf16[4,896,256]{2,1,0:T(8,128)(2,1)} async-done(((bf16[4,896,256]{2,1,0:T(8,128)(2,1)}), bf16[4,896,256]{2,1,0:T(8,128)(2,1)}, u32[]{:S(2)}, u32[]{:S(2)}) %all-to-all-start.2) | async-done | bytes 1835040 | tf_op jit(solution)/shard_map/all_to_all | solution.py:80
  265.9 3.5 %copy.28 = bf16[896,4,256]{0,2,1:T(8,128)(2,1)} copy(bf16[896,4,256]{2,0,1:T(8,128)(2,1)} %bitcast.14) | data formatting | bytes 3670016 | tf_op jit(solution)/shard_map/all_to_all | solution.py:80
  269.5 6.4 %fusion.22 = f32[1024,896]{1,0:T(8,128)} fusion(bf16[1024,1024]{1,0:T(8,128)(2,1)} %all-gather.9.cloned.1.call-done, bf16[896,1024]{0,1:T(8,128)(2,1)} %bitcast.62), kind=kOutput, calls=%fused_computation.56 | convolution fusion | flops 1879048192 | bytes 7602176 | tf_op jit(solution)/shard_map/dot_general | solution.py:8
  275.9 0.0 copy-done.4
  275.9 6.3 %add_convert_fusion = bf16[1024,896]{1,0:T(8,128)(2,1)} fusion(f32[1024,896]{1,0:T(8,128)} %fusion.22, bf16[1024,1024]{1,0:T(8,128)(2,1)} %all-gather.11.cloned.1.call-done, bf16[896,1024]{0,1:T(8,128)(2,1)S(1)} %bitcast.61), kind=kOutput, calls=%fused_computation.10 | convolution fusion | flops 1880883200 | bytes 9437184 | tf_op jit(solution)/shard_map/dot_general | solution.py:8
  282.1 5.6 %all-to-all-start.4 = ((bf16[8,128,896]{2,1,0:T(8,128)(2,1)}), bf16[8,128,896]{2,1,0:T(8,128)(2,1)}, u32[]{:S(2)}, u32[]{:S(2)}) async-start(bf16[8,128,896]{2,1,0:T(8,128)(2,1)} %bitcast.19), calls=%async_computation.4 | async-start | bytes 3670016 | tf_op jit(solution)/shard_map/all_to_all | solution.py:87
  287.8 0.1 reduce_sum.26
  287.9 0.1 copy.24
  288.0 0.0 copy-done.8
  288.0 0.2 copy.25
  288.2 0.0 slice-start
  288.2 6.6 %fusion.1 = bf16[1,3584,256]{2,1,0:T(8,128)(2,1)} fusion(bf16[1024,3584]{1,0:T(8,128)(2,1)} %bitcast.67, bf16[1024,256]{1,0:T(8,128)(2,1)S(1)} %copy-done.6), kind=kOutput, calls=%fused_computation.8 | convolution fusion | flops 1879965696 | bytes 9699328 | tf_op jit(solution)/shard_map/dot_general | solution.py:14
  294.9 6.6 %fusion = bf16[1,3584,256]{2,1,0:T(8,128)(2,1)} fusion(bf16[1024,3584]{1,0:T(8,128)(2,1)} %bitcast.68, bf16[1024,256]{1,0:T(8,128)(2,1)S(1)} %copy-done.5), kind=kOutput, calls=%fused_computation.7 | convolution fusion | flops 1879965696 | bytes 9699328 | tf_op jit(solution)/shard_map/dot_general | solution.py:14
  301.4 0.0 slice-done
  301.5 3.4 fusion.2
  304.8 25.4 %all-to-all-done.4 = bf16[8,128,896]{2,1,0:T(8,128)(2,1)} async-done(((bf16[8,128,896]{2,1,0:T(8,128)(2,1)}), bf16[8,128,896]{2,1,0:T(8,128)(2,1)}, u32[]{:S(2)}, u32[]{:S(2)}) %all-to-all-start.4) | async-done | bytes 1835040 | tf_op jit(solution)/shard_map/all_to_all | solution.py:87
  330.3 4.4 %gather_fusion.2 = bf16[512,896]{1,0:T(8,128)(2,1)S(1)} fusion(bf16[1024,896]{1,0:T(8,128)(2,1)} %bitcast.20, s32[1024]{0:T(1024)S(1)} %pad_clamp_fusion), kind=kCustom, calls=%fused_computation.2 | custom fusion | bytes 1837056 | tf_op jit(solution)/shard_map/jit(_take)/gather | solution.py:90
  334.7 1.3 gather.23
  336.0 4.3 %fusion.10 = bf16[256,896]{1,0:T(8,128)(2,1)} fusion(bf16[256,2,896]{2,1,0:T(2,128)(2,1)} %gather.23, pred[256,2]{1,0:T(8,128)(4,1)S(1)} %copy.25), kind=kLoop, calls=%fused_computation.26 | loop fusion | flops 688128 | bytes 1376768 | tf_op jit(solution)/shard_map/reduce_sum | solution.py:91
  (31 shorter events, 0.1 us)
Async XLA Ops:
  7.2 175.5 %copy-start = (bf16[1,256,3584]{2,1,0:T(8,128)(2,1)S(1)}, bf16[1,256,3584]{2,1,0:T(8,128)(2,1)}, u32[]{:S(2)}) copy-start(bf16[1,256,3584]{2,1,0:T(8,128)(2,1)} %param.13) | copy-start | bytes 5505028
  7.2 6.3 %copy-start.2 = (bf16[256,896]{1,0:T(8,128)(2,1)S(1)}, bf16[256,896]{1,0:T(8,128)(2,1)}, u32[]{:S(2)}) copy-start(bf16[256,896]{1,0:T(8,128)(2,1)} %param.7) | copy-start | bytes 1376260
  7.2 124.2 %all-gather.7.cloned.1.call-start = ((), (), s32[]{:S(2)}) async-start(), calls=%async_computation.6 | async-start | bytes 9175040 | tf_op jit(solution)/shard_map/all_gather | solution.py:73
  70.4 0.7 copy-start.9
  70.4 1.0 copy-start.7
  70.4 112.3 %all-gather.5.cloned.1.call-start = ((), (), s32[]{:S(2)}) async-start(), calls=%async_computation.5 | async-start | bytes 9175040 | tf_op jit(solution)/shard_map/all_gather | solution.py:74
  131.3 138.2 %all-gather.9.cloned.1.call-start = ((), (), s32[]{:S(2)}) async-start(), calls=%async_computation.7 | async-start | bytes 2621440 | tf_op jit(solution)/shard_map/all_gather | solution.py:84
  131.4 6.8 %copy-start.3 = (bf16[1,3584,256]{2,1,0:T(8,128)(2,1)S(1)}, bf16[1,3584,256]{2,1,0:T(8,128)(2,1)}, u32[]{:S(2)}) copy-start(bf16[1,3584,256]{2,1,0:T(8,128)(2,1)} %param.12) | copy-start | bytes 5505028
  131.4 6.8 %copy-start.10 = (bf16[8,128,3584]{2,1,0:T(8,128)(2,1)S(1)}, bf16[8,128,3584]{2,1,0:T(8,128)(2,1)}, u32[]{:S(2)}) copy-start(bf16[8,128,3584]{2,1,0:T(8,128)(2,1)} %all-gather.7.cloned.1.call-done) | copy-start | bytes 22020100
  189.6 37.7 %all-to-all-start.3 = ((bf16[4,896,256]{2,1,0:T(8,128)(2,1)}), bf16[4,896,256]{2,1,0:T(8,128)(2,1)S(1)}, u32[]{:S(2)}, u32[]{:S(2)}) async-start(bf16[4,896,256]{2,1,0:T(8,128)(2,1)} %bitcast.59), calls=%async_computation.3 | async-start | bytes 3670016 | tf_op jit(solution)/shard_map/all_to_all | solution.py:81
  193.2 82.6 %all-gather.11.cloned.1.call-start = ((), (), s32[]{:S(2)}) async-start(), calls=%async_computation.8 | async-start | bytes 2621440 | tf_op jit(solution)/shard_map/all_gather | solution.py:85
  227.3 38.6 %all-to-all-start.2 = ((bf16[4,896,256]{2,1,0:T(8,128)(2,1)}), bf16[4,896,256]{2,1,0:T(8,128)(2,1)}, u32[]{:S(2)}, u32[]{:S(2)}) async-start(bf16[4,896,256]{2,1,0:T(8,128)(2,1)} %bitcast.60), calls=%async_computation.2 | async-start | bytes 3670016 | tf_op jit(solution)/shard_map/all_to_all | solution.py:80
  269.5 6.4 %copy-start.4 = (bf16[896,4,256]{0,2,1:T(8,128)(2,1)S(1)}, bf16[896,4,256]{0,2,1:T(8,128)(2,1)}, u32[]{:S(2)}) copy-start(bf16[896,4,256]{0,2,1:T(8,128)(2,1)} %copy.29) | copy-start | bytes 5505028
  282.1 5.9 %copy-start.8 = (s32[256,2]{0,1:T(2,128)S(1)}, s32[256,2]{0,1:T(2,128)}, u32[]{:S(2)}) copy-start(s32[256,2]{0,1:T(2,128)} %param.9) | copy-start | bytes 6148
  282.1 6.1 %copy-start.6 = (bf16[1024,256]{1,0:T(8,128)(2,1)S(1)}, bf16[1024,256]{1,0:T(8,128)(2,1)}, u32[]{:S(2)}) copy-start(bf16[1024,256]{1,0:T(8,128)(2,1)} %get-tuple-element.4) | copy-start | bytes 1572868
  282.1 48.2 %all-to-all-start.4 = ((bf16[8,128,896]{2,1,0:T(8,128)(2,1)}), bf16[8,128,896]{2,1,0:T(8,128)(2,1)}, u32[]{:S(2)}, u32[]{:S(2)}) async-start(bf16[8,128,896]{2,1,0:T(8,128)(2,1)} %bitcast.19), calls=%async_computation.4 | async-start | bytes 3670016 | tf_op jit(solution)/shard_map/all_to_all | solution.py:87
  288.2 6.6 %copy-start.5 = (bf16[1024,256]{1,0:T(8,128)(2,1)S(1)}, bf16[1024,256]{1,0:T(8,128)(2,1)}, u32[]{:S(2)}) copy-start(bf16[1024,256]{1,0:T(8,128)(2,1)} %get-tuple-element.5) | copy-start | bytes 1572868
  288.2 13.2 %slice-start = ((s8[7340032]{0:T(1024)(128)(4,1)}), s8[4194304]{0:T(1024)(128)(4,1)S(1)}, s32[]{:S(2)}) async-start(s8[7340032]{0:T(1024)(128)(4,1)} %bitcast.71), calls=%async_computation.9 | async-start | bytes 8388608
  294.8 6.6 %slice-start.1 = ((s8[7340032]{0:T(1024)(128)(4,1)}), s8[3145728]{0:T(1024)(128)(4,1)S(1)}, s32[]{:S(2)}) async-start(s8[7340032]{0:T(1024)(128)(4,1)} %bitcast.71), calls=%async_computation.10 | async-start | bytes 6291456
  294.8 6.6 %copy-start.11 = (f32[1024,256]{1,0:T(8,128)S(1)}, f32[1024,256]{1,0:T(8,128)}, u32[]{:S(2)}) copy-start(f32[1024,256]{1,0:T(8,128)} %fusion.3) | copy-start | bytes 3145732
  294.8 6.6 %copy-start.12 = (f32[1024,256]{1,0:T(8,128)S(1)}, f32[1024,256]{1,0:T(8,128)}, u32[]{:S(2)}) copy-start(f32[1024,256]{1,0:T(8,128)} %fusion.5) | copy-start | bytes 3145732
  330.3 10.0 %copy-start.1 = (bf16[1,256,3584]{2,1,0:T(8,128)(2,1)S(1)}, bf16[1,256,3584]{2,1,0:T(8,128)(2,1)}, u32[]{:S(2)}) copy-start(bf16[1,256,3584]{2,1,0:T(8,128)(2,1)} %param.13) | copy-start | bytes 5505028
Sparse Core Ops, SparseCore 0:
  70.5 51.3 all-gather.6
  131.4 51.2 all-gather.4
  189.7 34.1 all-gather.8
  225.9 34.0 all-gather.10
where the time goes:
time: 348 us; the launch traced here: 347 us
  waiting for transfers between devices  133 us (38%)
  blocking collectives  95.5 us (27%)
  matrix products  45.9 us (13%)
  local copies, waits for them, and re-layouts  32.6 us (9%)
  starting transfers between devices  14 us (4%)
  between operations  14 us (4%)
  other arithmetic  12 us (3%)
    all_to_all x1, blocking collectives, per_device(): lax.all_to_all(x_send, 'ep', split_axis=0, concat_axis=0, tiled=True)  49.8 us
    all_to_all x1, blocking collectives, per_device(): lax.all_to_all(s_send, 'ep', split_axis=0, concat_axis=0, tiled=True)  45.7 us
    all_gather x1, waiting for transfers between devices, per_device(): lax.all_gather(s_recv, 'tp', axis=2, tiled=True)  41.5 us
    all_to_all x1, waiting for transfers between devices, per_device(): lax.all_to_all(up_cols, 'tp', split_axis=0, concat_axis=1, tiled=True)  33.5 us
    all_to_all x1, waiting for transfers between devices, per_device(): lax.all_to_all(gate_cols, 'tp', split_axis=0, concat_axis=1, tiled=True)  31.7 us
    all_to_all x1, waiting for transfers between devices, per_device(): lax.all_to_all(dx_rows.reshape(n_src, cap, quarter), 'ep', split_axis=0,...  25.4 us
    dot_general x3, matrix products, contract_last(): lax.dot_general(left, right, (((1,), (1,)), ((), ())), preferred_element_...  19.6 us
    dot_general x3, matrix products, contract_first(): lax.dot_general(left, right, (((0,), (0,)), ((), ())), preferred_element_...  16.6 us
  transfers between devices with their start and end apart: 7, of which 4 were waited for; matrix products, arithmetic and copies ran while one was open for 15% of the time, Pallas kernels for 0%

commit v1 on v0

v1 whole, which is shorter than its diff:
```python
import functools

import jax
import jax.numpy as jnp
from jax import lax
from jax.experimental import pallas as pl
from jax.experimental.pallas import tpu as pltpu
from jax.sharding import PartitionSpec as P

F32 = jnp.float32
BF16 = jnp.bfloat16


def mul(left, right):
    return jnp.dot(left, right, preferred_element_type=F32)


def contract_last(left, right):
    return lax.dot_general(left, right, (((1,), (1,)), ((), ())), preferred_element_type=F32)


def contract_first(left, right):
    return lax.dot_general(left, right, (((0,), (0,)), ((), ())), preferred_element_type=F32)


def kernel(
    n, tok, gout, code, prob, wg, wu, wd,
    g_tok, g_gate, g_up, g_down,
    stage, xs, dg, du, hid, dxp, dxr, dyr, back, acc,
    ep_s, ep_r, ya_s, ya_r, ma_s, ma_r, mb_s, mb_r, dm_s, dm_r, dy_s, dy_r, rt_s, rt_r,
):
    me = lax.axis_index("ep")
    t = lax.axis_index("tp")
    low = lax.rem(t, 2)
    high = t // 2
    mate = t + 1 - 2 * low
    across = lax.rem(t + 2, 4)
    cap, quarter = stage.shape[2], stage.shape[3]
    rows = tok.shape[0]

    barrier = pltpu.get_barrier_semaphore()

    def greet(j, carry):
        pl.semaphore_signal(barrier, inc=1, device_id={"ep": lax.rem(me + j, n)})
        return carry

    lax.fori_loop(1, n, greet, 0)
    pl.semaphore_signal(barrier, inc=1, device_id={"tp": mate})
    pl.semaphore_signal(barrier, inc=1, device_id={"tp": across})
    pl.semaphore_wait(barrier, n + 1)

    def copy(src, dst, send, recv, j, to):
        return pltpu.make_async_remote_copy(
            src_ref=src, dst_ref=dst, send_sem=send.at[j], recv_sem=recv.at[j], device_id=to
        )

    def ep_copy(j):
        return copy(stage.at[j], xs.at[j, t], ep_s, ep_r, j, {"ep": lax.rem(me + j, n)})

    def across_copy(j):
        return copy(xs.at[j, t], xs.at[j, t], ya_s, ya_r, j, {"tp": across})

    def mate_copy(j):
        return copy(xs.at[j, t], xs.at[j, t], ma_s, ma_r, j, {"tp": mate})

    def relay_copy(j):
        return copy(xs.at[j, across], xs.at[j, across], mb_s, mb_r, j, {"tp": mate})

    def part_copy(j):
        return copy(dxp.at[j, 1 - low], dxr.at[j], dm_s, dm_r, j, {"tp": mate})

    def half_copy(j):
        return copy(dxp.at[j, low, 1 - high], dyr.at[j], dy_s, dy_r, j, {"tp": across})

    def return_copy(j):
        return copy(
            dxp.at[j, low, high], back.at[j], rt_s, rt_r, j, {"ep": lax.rem(me - j + n, n)}
        )

    def chosen(j):
        expert = lax.rem(me + j, n)
        return lax.broadcasted_iota(jnp.int32, (cap, rows), 0) == code[expert]

    def pack(j):
        pick = chosen(j)
        share = jnp.sum(jnp.where(pick, prob[lax.rem(me + j, n)], 0.0), axis=1, keepdims=True)
        onehot = pick.astype(F32).astype(BF16)
        return mul(onehot, tok[...]).astype(BF16), (share * mul(onehot, gout[...])).astype(BF16)

    def send(j, carry):
        x_rows, s_rows = pack(j)
        stage[j, 0] = x_rows
        stage[j, 1] = s_rows
        ep_copy(j).start()
        return carry

    lax.fori_loop(1, n, send, 0)
    x_rows, s_rows = pack(0)
    xs[0, t, 0] = x_rows
    xs[0, t, 1] = s_rows

    def compute(j):
        gate = jnp.zeros((cap, wg.shape[1]), F32)
        upper, down = gate, gate
        for q in range(4):
            at = slice(q * quarter, (q + 1) * quarter)
            x = xs[j, q, 0]
            gate += mul(x, wg[at, :])
            upper += mul(x, wu[at, :])
            down += contract_last(xs[j, q, 1], wd[:, at])
        sigma = jax.nn.sigmoid(gate)
        active = gate * sigma
        hid[j] = (active * upper).astype(BF16)
        d_up = (down * active).astype(BF16)
        d_gate = (down * upper * sigma * (1.0 + gate * (1.0 - sigma))).astype(BF16)
        dg[j] = d_gate
        du[j] = d_up
        for q in range(4):
            at = slice(q * quarter, (q + 1) * quarter)
            part = contract_last(d_gate, wg[at, :]) + contract_last(d_up, wu[at, :])
            dxp[j, q % 2, q // 2] = part.astype(BF16)

    def step(i, carry):
        @pl.when(i < n)
        def _():
            @pl.when(i > 0)
            def _():
                ep_copy(i).wait_recv()

            across_copy(i).start()
            mate_copy(i).start()

        @pl.when(jnp.logical_and(i >= 1, i < n + 1))
        def _():
            j = i - 1
            across_copy(j).wait_recv()
            relay_copy(j).start()

        @pl.when(jnp.logical_and(i >= 2, i < n + 2))
        def _():
            j = i - 2
            mate_copy(j).wait_recv()
            relay_copy(j).wait_recv()
            compute(j)
            part_copy(j).start()

        @pl.when(jnp.logical_and(i >= 3, i < n + 3))
        def _():
            j = i - 3
            part_copy(j).wait_recv()
            for h in range(2):
                dxp[j, low, h] = (dxp[j, low, h].astype(F32) + dxr[j, h].astype(F32)).astype(BF16)
            half_copy(j).start()

        @pl.when(i >= 4)
        def _():
            j = i - 4
            half_copy(j).wait_recv()
            total = (dxp[j, low, high].astype(F32) + dyr[j].astype(F32)).astype(BF16)

            @pl.when(j == 0)
            def _():
                back[0] = total

            @pl.when(j > 0)
            def _():
                dxp[j, low, high] = total
                return_copy(j).start()

        return carry

    lax.fori_loop(0, n + 4, step, 0)

    def grads(q, carry):
        at = pl.ds(pl.multiple_of(q * quarter, 128), quarter)
        x = xs[:, q, 0].reshape(n * cap, quarter)
        g_gate[at, :] = contract_first(x, dg[...].reshape(n * cap, -1)).astype(BF16)
        g_up[at, :] = contract_first(x, du[...].reshape(n * cap, -1)).astype(BF16)
        s = xs[:, q, 1].reshape(n * cap, quarter)
        g_down[:, at] = contract_first(hid[...].reshape(n * cap, -1), s).astype(BF16)
        return carry

    lax.fori_loop(0, 4, grads, 0)

    acc[...] = contract_first(chosen(0).astype(F32).astype(BF16), back[0])

    def gather(j, carry):
        return_copy(j).wait_recv()
        acc[...] += contract_first(chosen(j).astype(F32).astype(BF16), back[j])
        return carry

    lax.fori_loop(1, n, gather, 0)
    g_tok[...] = acc[...].astype(BF16)

    def drain(j, carry):
        @pl.when(j > 0)
        def _():
            ep_copy(j).wait_send()
            return_copy(j).wait_send()

        across_copy(j).wait_send()
        mate_copy(j).wait_send()
        relay_copy(j).wait_send()
        part_copy(j).wait_send()
        half_copy(j).wait_send()
        return carry

    lax.fori_loop(0, n, drain, 0)


def per_device(tokens, grad_out, route_ids, route_probs, w_gate, w_up, w_down):
    n = lax.axis_size("ep")
    tp = lax.axis_size("tp")
    rows, quarter = tokens.shape
    top = route_ids.shape[1]
    width, ff = w_gate.shape[1:]
    cap = max(2, 2 * rows * top // n)
    experts = jnp.arange(n, dtype=jnp.int32)[:, None]
    named = [route_ids[:, k][None, :] == experts for k in range(top)]
    prob = sum(jnp.where(named[k], route_probs[:, k][None, :], 0.0) for k in range(top))
    mask = functools.reduce(jnp.logical_or, named)
    earlier = jnp.arange(rows)[:, None] < jnp.arange(rows)[None, :]
    rank = mul(mask.astype(BF16), earlier.astype(BF16)).astype(jnp.int32)
    code = jnp.where(mask, rank, -1)
    sems = pltpu.SemaphoreType.DMA((n,))
    vmem = pl.BlockSpec(memory_space=pltpu.VMEM)
    g_tok, g_gate, g_up, g_down = pl.pallas_call(
        functools.partial(kernel, n),
        out_shape=(
            jax.ShapeDtypeStruct((rows, quarter), BF16),
            jax.ShapeDtypeStruct((width, ff), BF16),
            jax.ShapeDtypeStruct((width, ff), BF16),
            jax.ShapeDtypeStruct((ff, width), BF16),
        ),
        in_specs=[vmem] * 7,
        out_specs=(vmem,) * 4,
        scratch_shapes=[
            pltpu.VMEM((n, 2, cap, quarter), BF16),
            pltpu.VMEM((n, tp, 2, cap, quarter), BF16),
            pltpu.VMEM((n, cap, ff), BF16),
            pltpu.VMEM((n, cap, ff), BF16),
            pltpu.VMEM((n, cap, ff), BF16),
            pltpu.VMEM((n, 2, 2, cap, quarter), BF16),
            pltpu.VMEM((n, 2, cap, quarter), BF16),
            pltpu.VMEM((n, cap, quarter), BF16),
            pltpu.VMEM((n, cap, quarter), BF16),
            pltpu.VMEM((rows, quarter), F32),
        ]
        + [sems] * 14,
        compiler_params=pltpu.CompilerParams(
            collective_id=0, has_side_effects=True, vmem_limit_bytes=60 * 1024 * 1024
        ),
    )(
        tokens, grad_out, code.reshape(n, 1, rows), prob.reshape(n, 1, rows),
        w_gate[0], w_up[0], w_down[0],
    )
    return g_tok, g_gate[None], g_up[None], g_down[None]


def solution(mesh):
    placed = (
        P("ep", "tp"),
        P("ep", "tp"),
        P("ep", None),
        P("ep", None),
        P("ep", None, "tp"),
        P("ep", None, "tp"),
        P("ep", "tp", None),
    )
    return jax.shard_map(
        per_device,
        mesh=mesh,
        in_specs=placed,
        out_specs=(P("ep", "tp"), P("ep", None, "tp"), P("ep", None, "tp"), P("ep", "tp", None)),
        check_vma=False,
    )
```

time: 348 us -> 195 us (0.56)
  Pallas kernels: 0 us -> 183 us
  waiting for transfers between devices: 133 us -> 0 us
  blocking collectives: 95.5 us -> 0 us
  matrix products: 45.9 us -> 0.15 us
  local copies, waits for them, and re-layouts: 32.6 us -> 10.3 us
  starting transfers between devices: 14 us -> 0 us
  between operations: 14 us -> 0.64 us
  other arithmetic: 12 us -> 0.61 us
    pallas_call x0 -> x1, Pallas kernels: none -> 183 us  [per_device(): pl.pallas_call(functools.partial(kernel, n), out_shape=(jax.ShapeDtypeStr...]
    all_to_all x2 -> x0, blocking collectives: 95.5 us -> none  [the longest x1 49.8 us: per_device(): lax.all_to_all(x_send, 'ep', split_axis=0, concat_axis=0, tiled=True)]
    all_to_all x3 -> x0, waiting for transfers between devices: 90.7 us -> none  [the longest x1 33.5 us: per_device(): lax.all_to_all(up_cols, 'tp', split_axis=0, concat_axis=1, tiled=True)]
    dot_general x8 -> x1, matrix products: 45.9 us -> 0.15 us  [mul(): return jnp.dot(left, right, preferred_element_type=F32)]
    all_gather x4 -> x0, waiting for transfers between devices: 41.5 us -> none  [the longest x1 41.5 us: per_device(): lax.all_gather(s_recv, 'tp', axis=2, tiled=True)]
    gather x4 -> x0, local copies, waits for them, and re-layouts: 16.2 us -> none  [the longest x2 5.67 us: per_device(): per_route = jnp.take(back_slots.reshape(n_src * cap, quarter), slot, axis=0)]
    all_to_all x3 -> x0, starting transfers between devices: 13.8 us -> none  [the longest x1 5.64 us: per_device(): lax.all_to_all(dx_rows.reshape(n_src, cap, quarter), 'ep', split_axis=0,...]
    unnamed x32 -> x8, local copies, waits for them, and re-layouts: 1.69 us -> 8.19 us
  transfers between devices with their start and end apart: 7 -> 0, of which waited for: 4 -> 0; matrix products, arithmetic and copies ran while one was open for 15% -> 0% of each run, Pallas kernels for 0% -> 0%
where the time goes in v1:
time: 195 us; the launch traced here: 194 us
  Pallas kernels  183 us (94%)
  local copies, waits for them, and re-layouts  10.3 us (5%)
    pallas_call x1, Pallas kernels, per_device(): pl.pallas_call(functools.partial(kernel, n), out_shape=(jax.ShapeDtypeStr...  183 us
    unnamed x8, local copies, waits for them, and re-layouts  8.19 us

profile of v1, /device:TPU:0, one launch (start us, length us, event | category | flops | bytes accessed | tf_op | source)
XLA Modules:
  0.0 194.3 jit_solution(17222381681082605896)
XLA Ops:
  0.6 0.8 fusion.7
  1.4 0.8 fusion.6
  2.2 0.6 fusion.1.prob
  2.8 0.2 fusion
  2.9 0.6 reshape.155.code
  3.5 182.5 %shard_map.102 = (bf16[256,896]{1,0:T(8,128)(2,1)}, bf16[3584,256]{1,0:T(8,128)(2,1)}, bf16[3584,256]{1,0:T(8,128)(2,1)}, bf16[256,3584]{1,0:T(8,128)(2,1)}) custom-call(bf16[256,896]{1,0:T(8,128)(2,1)} %tok.1, bf16[256,896]{1,0:T(8,128)(2,1)} %gout.1, s32[8,1,256]{2,1,0:T(1,128)} %reshape.155.code, f32[8,1,256]{2,1,0:T(1,128)} %fusion.1.prob, ...), custom_call_target="tpu_custom_call" | custom-call | tf_op jit(solution)/shard_map/pallas_call | solution.py:227
  186.1 1.8 copy.15
  187.9 0.0 copy-start.1
  187.9 3.0 %copy.16 = bf16[1,3584,256]{2,1,0:T(8,128)(2,1)} copy(bf16[1,3584,256]{2,1,0:T(8,128)(2,1)} %bitcast.12) | data formatting | bytes 3670016
  190.9 0.0 copy-done.1
  190.9 0.0 copy-start
  190.9 1.2 copy.17
  192.1 0.9 copy-done
  193.1 1.2 copy.18
Async XLA Ops:
  187.9 3.0 %copy-start.1 = (bf16[3584,256]{1,0:T(8,128)(2,1)S(1)}, bf16[3584,256]{1,0:T(8,128)(2,1)}, u32[]{:S(2)}) copy-start(bf16[3584,256]{1,0:T(8,128)(2,1)} %get-tuple-element.10) | copy-start | bytes 5505028
  190.9 2.2 %copy-start = (bf16[256,3584]{1,0:T(8,128)(2,1)S(1)}, bf16[256,3584]{1,0:T(8,128)(2,1)}, u32[]{:S(2)}) copy-start(bf16[256,3584]{1,0:T(8,128)(2,1)} %get-tuple-element.11) | copy-start | bytes 5505028

commit v2 on v1

--- a/solution.py
+++ b/solution.py
@@ -77,6 +77,10 @@
             dxp.at[j, low, high], back.at[j], rt_s, rt_r, j, {"ep": lax.rem(me - j + n, n)}
         )
 
+    def near(k):
+        odd = lax.rem(k, 2)
+        return odd * lax.div(k + 1, 2) + (1 - odd) * lax.rem(n - lax.div(k, 2), n)
+
     def chosen(j):
         expert = lax.rem(me + j, n)
         return lax.broadcasted_iota(jnp.int32, (cap, rows), 0) == code[expert]
@@ -87,7 +91,8 @@
         onehot = pick.astype(F32).astype(BF16)
         return mul(onehot, tok[...]).astype(BF16), (share * mul(onehot, gout[...])).astype(BF16)
 
-    def send(j, carry):
+    def send(k, carry):
+        j = near(k)
         x_rows, s_rows = pack(j)
         stage[j, 0] = x_rows
         stage[j, 1] = s_rows
@@ -120,67 +125,74 @@
             part = contract_last(d_gate, wg[at, :]) + contract_last(d_up, wu[at, :])
             dxp[j, q % 2, q // 2] = part.astype(BF16)
 
-    def step(i, carry):
-        @pl.when(i < n)
-        def _():
-            @pl.when(i > 0)
-            def _():
-                ep_copy(i).wait_recv()
-
-            across_copy(i).start()
-            mate_copy(i).start()
-
-        @pl.when(jnp.logical_and(i >= 1, i < n + 1))
-        def _():
-            j = i - 1
-            across_copy(j).wait_recv()
-            relay_copy(j).start()
-
-        @pl.when(jnp.logical_and(i >= 2, i < n + 2))
-        def _():
-            j = i - 2
-            mate_copy(j).wait_recv()
-            relay_copy(j).wait_recv()
-            compute(j)
-            part_copy(j).start()
-
-        @pl.when(jnp.logical_and(i >= 3, i < n + 3))
-        def _():
-            j = i - 3
-            part_copy(j).wait_recv()
-            for h in range(2):
-                dxp[j, low, h] = (dxp[j, low, h].astype(F32) + dxr[j, h].astype(F32)).astype(BF16)
-            half_copy(j).start()
-
-        @pl.when(i >= 4)
-        def _():
-            j = i - 4
-            half_copy(j).wait_recv()
-            total = (dxp[j, low, high].astype(F32) + dyr[j].astype(F32)).astype(BF16)
-
-            @pl.when(j == 0)
-            def _():
-                back[0] = total
-
-            @pl.when(j > 0)
-            def _():
-                dxp[j, low, high] = total
-                return_copy(j).start()
-
-        return carry
-
-    lax.fori_loop(0, n + 4, step, 0)
-
-    def grads(q, carry):
+    def grads(q):
         at = pl.ds(pl.multiple_of(q * quarter, 128), quarter)
         x = xs[:, q, 0].reshape(n * cap, quarter)
         g_gate[at, :] = contract_first(x, dg[...].reshape(n * cap, -1)).astype(BF16)
         g_up[at, :] = contract_first(x, du[...].reshape(n * cap, -1)).astype(BF16)
         s = xs[:, q, 1].reshape(n * cap, quarter)
         g_down[:, at] = contract_first(hid[...].reshape(n * cap, -1), s).astype(BF16)
-        return carry
-
-    lax.fori_loop(0, 4, grads, 0)
+
+    def step(i, carry):
+        @pl.when(i >= 4)
+        def _():
+            j = near(i - 4)
+            half_copy(j).wait_recv()
+            total = (dxp[j, low, high].astype(F32) + dyr[j].astype(F32)).astype(BF16)
+
+            @pl.when(j == 0)
+            def _():
+                back[0] = total
+
+            @pl.when(j > 0)
+            def _():
+                dxp[j, low, high] = total
+                return_copy(j).start()
+
+        @pl.when(jnp.logical_and(i >= 3, i < n + 3))
+        def _():
+            j = near(i - 3)
+            part_copy(j).wait_recv()
+            for h in range(2):
+                dxp[j, low, h] = (dxp[j, low, h].astype(F32) + dxr[j, h].astype(F32)).astype(BF16)
+            half_copy(j).start()
+
+        @pl.when(jnp.logical_and(i >= 2, i < n + 2))
+        def _():
+            j = near(i - 2)
+            mate_copy(j).wait_recv()
+            relay_copy(j).wait_recv()
+            compute(j)
+            part_copy(j).start()
+
+        @pl.when(jnp.logical_and(i >= 1, i < n + 1))
+        def _():
+            j = near(i - 1)
+            across_copy(j).wait_recv()
+            relay_copy(j).start()
+
+        @pl.when(i < n)
+        def _():
+            @pl.when(i > 0)
+            def _():
+                ep_copy(near(i)).wait_recv()
+
+            across_copy(near(i)).start()
+            mate_copy(near(i)).start()
+
+        @pl.when(i >= n + 2)
+        def _():
+            grads(i - n - 2)
+
+        return carry
+
+    lax.fori_loop(0, n + 4, step, 0)
+
+    def rest(q, carry):
+        grads(q)
+        return carry
+
+    lax.fori_loop(2, 4, rest, 0)
 
     acc[...] = contract_first(chosen(0).astype(F32).astype(BF16), back[0])
 

time: 195 us -> 172 us (0.88)
  Pallas kernels: 183 us -> 160 us
    pallas_call x1, Pallas kernels: 183 us -> 160 us  [per_device(): pl.pallas_call(functools.partial(kernel, n), out_shape=(jax.ShapeDtypeStr...]
where the time goes in v2:
time: 172 us
  Pallas kernels  160 us (93%)
  local copies, waits for them, and re-layouts  10.3 us (6%)
    pallas_call x1, Pallas kernels, per_device(): pl.pallas_call(functools.partial(kernel, n), out_shape=(jax.ShapeDtypeStr...  160 us
    unnamed x8, local copies, waits for them, and re-layouts  8.19 us

profile of v2, /device:TPU:0, one launch (start us, length us, event | category | flops | bytes accessed | tf_op | source)
XLA Modules:
  0.0 171.6 jit_solution(1521659475068453747)
XLA Ops:
  0.6 0.8 fusion.7
  1.4 0.8 fusion.6
  2.2 0.6 fusion.1.prob
  2.8 0.2 fusion
  2.9 0.6 reshape.155.code
  3.5 159.9 %shard_map.102 = (bf16[256,896]{1,0:T(8,128)(2,1)}, bf16[3584,256]{1,0:T(8,128)(2,1)}, bf16[3584,256]{1,0:T(8,128)(2,1)}, bf16[256,3584]{1,0:T(8,128)(2,1)}) custom-call(bf16[256,896]{1,0:T(8,128)(2,1)} %tok.1, bf16[256,896]{1,0:T(8,128)(2,1)} %gout.1, s32[8,1,256]{2,1,0:T(1,128)} %reshape.155.code, f32[8,1,256]{2,1,0:T(1,128)} %fusion.1.prob, ...), custom_call_target="tpu_custom_call" | custom-call | tf_op jit(solution)/shard_map/pallas_call | solution.py:239
  163.4 1.8 %copy.15 = bf16[256,896]{1,0:T(8,128)(2,1)} copy(bf16[256,896]{1,0:T(8,128)(2,1)} %get-tuple-element.20) | data formatting | bytes 917504
  165.3 0.0 copy-start.1
  165.3 3.0 %copy.16 = bf16[1,3584,256]{2,1,0:T(8,128)(2,1)} copy(bf16[1,3584,256]{2,1,0:T(8,128)(2,1)} %bitcast.12) | data formatting | bytes 3670016
  168.2 0.0 copy-done.1
  168.2 0.0 copy-start
  168.2 1.2 copy.17
  169.5 0.9 copy-done
  170.4 1.2 copy.18
Async XLA Ops:
  165.3 3.0 %copy-start.1 = (bf16[3584,256]{1,0:T(8,128)(2,1)S(1)}, bf16[3584,256]{1,0:T(8,128)(2,1)}, u32[]{:S(2)}) copy-start(bf16[3584,256]{1,0:T(8,128)(2,1)} %get-tuple-element.10) | copy-start | bytes 5505028
  168.2 2.2 %copy-start = (bf16[256,3584]{1,0:T(8,128)(2,1)S(1)}, bf16[256,3584]{1,0:T(8,128)(2,1)}, u32[]{:S(2)}) copy-start(bf16[256,3584]{1,0:T(8,128)(2,1)} %get-tuple-element.11) | copy-start | bytes 5505028
